TPU v7x, 512 devices: a whole 4x8x8 slice. The times are simulated.
512 devices in a mesh: member: 16 (over x_lo, y), tile: 32 (over z, x_hi, core).
Axes of the slice: x: 4 (x_hi: 2, x_lo: 2; x = x_hi * 2 + x_lo), y: 8, z: 8, core: 2. Of those that a mesh axis runs over, the one named last changes fastest.
Arguments:
- density: float32 [16, 6, 512, 512], P('member', None, 'tile'), may hold values from 0.05 to 5
- scaling: float32 [16, 6, 512, 512], P('member', None, 'tile'), may hold values from 0.2 to 5
- member_weights: float32 [16], P('member'), may hold values from 0.5 to 11
- seams: int32 [3, 4, 6], replicated, may hold values from 0 to 5, as said below
Outputs:
- new_scaling: float32 [16, 6, 512, 512], P('member', None, 'tile')
- dual_scaling: float32 [16, 6, 512, 512], P('member', None, 'tile')
- barycenter: float32 [6, 512, 512], P(None, 'tile')
Inputs may be any that keep to these rules, and one draw needn't show every extreme that they name: Edges are numbered 0 first row, 1 last row, 2 first column, 3 last column. The table describes the six faces of a cube, each face's frame turned or mirrored: seams[0, e, f] is the face across edge e of face f, seams[1, e, f] the edge of that face which meets it, and the relation is symmetric; seams[2, e, f] is 1 where positions along the seam run opposite ways on the two faces, and the same from both sides.
All inputs are finite; a program needn't handle non-finite values.
Results may differ from a plain program's by a relative error of at most 0.00007.
Values sent between devices are 32-bit elements; how exact they have to be, the bound alone decides.
No kernel may reach another device: no remote copies, remote signals or barrier semaphores. Data moves between devices by JAX's collectives and lax.ppermute only.
A program may use at most 64 MiB of HBM per device.

v0:
```python
import jax
import jax.numpy as jnp
from jax import lax
from jax.sharding import PartitionSpec as P

STEPS = 4
KAPPA = 0.24


def with_halo(block, sides, width):
    for axis, dim in sides:
        count = lax.axis_size(axis)
        forward = [(i, i + 1) for i in range(count - 1)]
        backward = [(target, source) for source, target in forward]
        low = lax.ppermute(
            lax.slice_in_dim(block, block.shape[dim] - width, None, axis=dim), axis, forward
        )
        high = lax.ppermute(lax.slice_in_dim(block, 0, width, axis=dim), axis, backward)
        block = jnp.concatenate([low, block, high], axis=dim)
    return block


def body(density, scaling, member_weights, seams):
    tiles = lax.axis_size("tile")
    position = lax.axis_index("tile")
    members = scaling.shape[0]
    faces = scaling.shape[1]
    rows = scaling.shape[2]
    side = scaling.shape[3]
    is_first = (position == 0).astype(jnp.float32)
    is_last = (position == tiles - 1).astype(jnp.float32)
    slots = jnp.arange(4 * faces, dtype=jnp.int32)
    selectors = []
    for edge_id in range(4):
        wanted = seams[0, edge_id] * 4 + seams[1, edge_id]
        selectors.append((wanted[:, None] == slots[None, :]).astype(jnp.float32))

    def edge_table(field):
        first_row = field[:, :, 0, :] * is_first
        last_row = field[:, :, -1, :] * is_last
        empty = jnp.zeros((members, faces, 2, side), jnp.float32)
        column_pieces = jnp.stack([field[:, :, :, 0], field[:, :, :, -1]], axis=2)
        placed = lax.dynamic_update_slice_in_dim(empty, column_pieces, position * rows, 3)
        local = jnp.concatenate([jnp.stack([first_row, last_row], axis=2), placed], axis=2)
        return lax.psum(local, "tile")

    def ghost(table, edge_id):
        flat = table.reshape(members, faces * 4, side)
        taken = jnp.einsum("fq,mqn->mfn", selectors[edge_id], flat, precision=lax.Precision.HIGHEST)
        return jnp.where((seams[2, edge_id] == 1)[None, :, None], taken[..., ::-1], taken)

    def diffuse(field):
        widened = with_halo(field, (("tile", 2),), 1)
        table = edge_table(field)
        upper = ghost(table, 0)
        lower = ghost(table, 1)
        start = position * rows
        left = lax.dynamic_slice_in_dim(ghost(table, 2), start, rows, 2)
        right = lax.dynamic_slice_in_dim(ghost(table, 3), start, rows, 2)
        top_row = jnp.where(position == 0, upper, widened[:, :, 0, :])
        bottom_row = jnp.where(position == tiles - 1, lower, widened[:, :, -1, :])
        widened = jnp.concatenate(
            [top_row[:, :, None, :], field, bottom_row[:, :, None, :]], axis=2
        )
        vertical = widened[:, :, :-2, :] + widened[:, :, 2:, :]
        lateral = jnp.concatenate([left[..., None], field[..., :-1]], axis=3) + jnp.concatenate(
            [field[..., 1:], right[..., None]], axis=3
        )
        return field + KAPPA * (vertical + lateral - 4.0 * field)

    def kernel(field):
        for counter in range(STEPS):
            field = diffuse(field)
        return field

    dual_scaling = density / kernel(scaling)
    marginal = scaling * kernel(dual_scaling)
    log_marginal = jnp.log(marginal)
    weighted = jnp.einsum(
        "k,kfrc->frc", member_weights, log_marginal, precision=lax.Precision.HIGHEST
    )
    weight_local = jnp.sum(member_weights)
    summed, weight_sum = lax.psum((weighted, weight_local), "member")
    barycenter = jnp.exp(summed / weight_sum)
    new_scaling = scaling * barycenter[None] / marginal
    return (new_scaling, dual_scaling, barycenter)


def solution(mesh):
    return jax.shard_map(
        body,
        mesh=mesh,
        in_specs=(
            P("member", None, "tile", None),
            P("member", None, "tile", None),
            P("member"),
            P(),
        ),
        out_specs=(
            P("member", None, "tile", None),
            P("member", None, "tile", None),
            P(None, "tile", None),
        ),
        check_vma=False,
    )
```

profile of v0, /device:TPU:4, one launch (start us, length us, event | category | flops | bytes accessed | tf_op | source)
XLA Modules:
  0.0 1329.6 jit_solution(210642740823785259)
XLA Ops:
  7.2 1.1 copy.123
  8.4 1.9 collective-permute-start
  10.3 5.1 collective-permute-start.1
  15.9 1.0 dynamic_update_slice.24
  17.0 131.4 %psum.70 = f32[24,512]{1,0:T(8,128)S(1)} all-reduce(f32[24,512]{1,0:T(8,128)S(1)} %reshape.773), channel_id=1, replica_groups=mesh['member'=16,'tile'=32] {'tile'}, use_global_device_ids=true, to_apply=%region_0.0 | all-reduce | flops 12288 | bytes 98304 | tf_op jit(solution)/shard_map/psum | solution.py:45
  150.6 0.3 rev.96
  152.2 1.0 dynamic_update_slice.25
  153.3 127.9 %psum.71 = f32[24,512]{1,0:T(8,128)S(1)} all-reduce(f32[24,512]{1,0:T(8,128)S(1)} %reshape.774), channel_id=1, replica_groups=mesh['member'=16,'tile'=32] {'tile'}, use_global_device_ids=true, to_apply=%region_1.2 | all-reduce | flops 12288 | bytes 98304 | tf_op jit(solution)/shard_map/psum | solution.py:45
  281.9 1.9 collective-permute-start.2
  283.8 5.1 collective-permute-start.3
  291.5 1.0 dynamic_update_slice.26
  292.6 125.8 %psum.72 = f32[24,512]{1,0:T(8,128)S(1)} all-reduce(f32[24,512]{1,0:T(8,128)S(1)} %reshape.775), channel_id=1, replica_groups=mesh['member'=16,'tile'=32] {'tile'}, use_global_device_ids=true, to_apply=%region_2.3 | all-reduce | flops 12288 | bytes 98304 | tf_op jit(solution)/shard_map/psum | solution.py:45
  419.1 1.9 collective-permute-start.4
  421.0 5.1 collective-permute-start.5
  426.2 0.3 rev.106
  428.7 1.0 dynamic_update_slice.27
  429.8 125.8 %psum.73 = f32[24,512]{1,0:T(8,128)S(1)} all-reduce(f32[24,512]{1,0:T(8,128)S(1)} %reshape.776), channel_id=1, replica_groups=mesh['member'=16,'tile'=32] {'tile'}, use_global_device_ids=true, to_apply=%region_3.4 | all-reduce | flops 12288 | bytes 98304 | tf_op jit(solution)/shard_map/psum | solution.py:45
  556.3 1.9 collective-permute-start.6
  558.2 5.1 collective-permute-start.7
  566.0 1.0 dynamic_update_slice.28
  567.1 130.9 %psum.74 = f32[24,512]{1,0:T(8,128)S(1)} all-reduce(f32[24,512]{1,0:T(8,128)S(1)} %reshape.777), channel_id=1, replica_groups=mesh['member'=16,'tile'=32] {'tile'}, use_global_device_ids=true, to_apply=%region_4.5 | all-reduce | flops 12288 | bytes 98304 | tf_op jit(solution)/shard_map/psum | solution.py:45
  698.8 3.8 collective-permute-start.8
  702.6 3.3 collective-permute-start.9
  705.8 0.3 rev.114
  707.7 2.1 collective-permute-done.9
  710.5 1.0 dynamic_update_slice.29
  711.6 133.7 %psum.75 = f32[24,512]{1,0:T(8,128)S(1)} all-reduce(f32[24,512]{1,0:T(8,128)S(1)} %reshape.778), channel_id=1, replica_groups=mesh['member'=16,'tile'=32] {'tile'}, use_global_device_ids=true, to_apply=%region_5.6 | all-reduce | flops 12288 | bytes 98304 | tf_op jit(solution)/shard_map/psum | solution.py:45
  846.0 3.5 collective-permute-start.10
  849.5 3.6 collective-permute-start.11
  854.9 1.8 collective-permute-done.11
  857.4 1.0 dynamic_update_slice.30
  858.6 133.7 %psum.76 = f32[24,512]{1,0:T(8,128)S(1)} all-reduce(f32[24,512]{1,0:T(8,128)S(1)} %reshape.779), channel_id=1, replica_groups=mesh['member'=16,'tile'=32] {'tile'}, use_global_device_ids=true, to_apply=%region_6.7 | all-reduce | flops 12288 | bytes 98304 | tf_op jit(solution)/shard_map/psum | solution.py:45
  993.0 3.5 collective-permute-start.12
  996.5 3.7 collective-permute-start.13
  1002.1 1.7 collective-permute-done.13
  1004.4 1.0 dynamic_update_slice.31
  1005.5 133.7 %psum.77 = f32[24,512]{1,0:T(8,128)S(1)} all-reduce(f32[24,512]{1,0:T(8,128)S(1)} %reshape.780), channel_id=1, replica_groups=mesh['member'=16,'tile'=32] {'tile'}, use_global_device_ids=true, to_apply=%region_7.8 | all-reduce | flops 12288 | bytes 98304 | tf_op jit(solution)/shard_map/psum | solution.py:45
  1139.9 3.5 collective-permute-start.14
  1143.5 3.6 collective-permute-start.15
  1147.0 0.3 rev.126
  1148.9 1.8 collective-permute-done.15
  1150.8 1.0 multiply_bitcast_fusion
  1151.8 36.2 %psum.79 = f32[]{:T(128)} all-reduce(f32[]{:T(128)} %bitcast.118), channel_id=1, replica_groups=mesh['member'=16,'tile'=32] {'member'}, use_global_device_ids=true, to_apply=%region_9.10 | all-reduce | flops 1 | bytes 8 | tf_op jit(solution)/shard_map/psum | solution.py:83
  1188.0 0.8 copy.125
  1188.8 130.6 %all-reduce.2.cloned.1.call-done = f32[6,16,512]{2,0,1:T(8,128)} async-done(((f32[6,16,512]{2,0,1:T(8,128)}), f32[6,16,512]{2,0,1:T(8,128)}) %all-reduce.2.cloned.1.call-update) | async-done | bytes 196624 | tf_op jit(solution)/shard_map/psum | solution.py:83
  1319.4 1.8 fusion.42
  1321.2 0.8 copy.124
  1322.0 0.8 copy.126
  (240 shorter events, 24.3 us)
Async XLA Ops:
  7.2 1312.2 %all-reduce.2.cloned.1.call-start = ((), (), s32[]{:S(2)}) async-start(), calls=%async_computation | async-start | bytes 524288 | tf_op jit(solution)/shard_map/psum | solution.py:83
  7.2 8.3 copy-start
  8.3 7.1 copy-start.2
  8.4 143.0 %collective-permute-start = (f32[1,6,1,512]{3,1,2,0:T(8,128)S(1)}, f32[1,6,1,512]{3,1,2,0:T(8,128)S(1)}, u32[]{:S(2)}, u32[]{:S(2)}) collective-permute-start(f32[1,6,1,512]{3,1,2,0:T(8,128)S(1)} %get-tuple-element.73), channel_id=1, source_target_pairs={{0,1},{1,2},{2,3},{3,4},{4,5},{5,6},{6,7},{7,8},{8,9},{9,10},{10,1... | collective-permute-start | bytes 36872 | tf_op jit(solution)/shard_map/ppermute | solution.py:15
  10.3 141.2 %collective-permute-start.1 = (f32[1,6,1,512]{3,1,2,0:T(8,128)S(1)}, f32[1,6,1,512]{3,1,2,0:T(8,128)S(1)}, u32[]{:S(2)}, u32[]{:S(2)}) collective-permute-start(f32[1,6,1,512]{3,1,2,0:T(8,128)S(1)} %get-tuple-element.76), channel_id=1, source_target_pairs={{1,0},{2,1},{3,2},{4,3},{5,4},{6,5},{7,6},{8,7},{9,8},{10,9},{11,1... | collective-permute-start | bytes 36872 | tf_op jit(solution)/shard_map/ppermute | solution.py:18
  281.9 8.8 collective-permute-start.2
  283.8 7.0 collective-permute-start.3
  419.1 8.8 collective-permute-start.4
  421.0 7.0 collective-permute-start.5
  556.3 8.9 collective-permute-start.6
  558.2 7.0 collective-permute-start.7
  564.1 1.2 copy-start.1
  698.8 8.8 collective-permute-start.8
  702.6 7.3 collective-permute-start.9
  846.0 8.8 collective-permute-start.10
  849.5 7.3 collective-permute-start.11
  993.0 9.0 collective-permute-start.12
  996.5 7.3 collective-permute-start.13
  1139.9 8.8 collective-permute-start.14
  1143.5 7.3 collective-permute-start.15
Sparse Core Ops, SparseCore 0:
  1151.9 167.4 all-reduce.1
where the time goes:
time: 1330 us
  blocking collectives  1080 us (81%)
  waiting for transfers between devices  138 us (10%)
  starting transfers between devices  56.8 us (4%)
  local copies, waits for them, and re-layouts  27 us (2%)
  between operations  15.7 us (1%)
    psum x8, blocking collectives, edge_table(): return lax.psum(local, 'tile')  1040 us
    psum x1, waiting for transfers between devices, body(): summed, weight_sum = lax.psum((weighted, weight_local), 'member')  131 us
    psum x1, blocking collectives, body(): summed, weight_sum = lax.psum((weighted, weight_local), 'member')  36.2 us
    ppermute x8, starting transfers between devices, with_halo(): lax.ppermute(lax.slice_in_dim(block, 0, width, axis=dim), axis, backward)  34.7 us
  transfers between devices with their start and end apart: 17, of which 5 were waited for; matrix products, arithmetic and copies ran while one was open for 1% of the time, Pallas kernels for 0%

commit v1 on v0

--- a/solution.py
+++ b/solution.py
@@ -42,7 +42,7 @@
         column_pieces = jnp.stack([field[:, :, :, 0], field[:, :, :, -1]], axis=2)
         placed = lax.dynamic_update_slice_in_dim(empty, column_pieces, position * rows, 3)
         local = jnp.concatenate([jnp.stack([first_row, last_row], axis=2), placed], axis=2)
-        return lax.psum(local, "tile")
+        return jnp.sum(lax.all_gather(local, "tile"), axis=0)
 
     def ghost(table, edge_id):
         flat = table.reshape(members, faces * 4, side)

time: 1330 us -> 865 us (0.65)
  blocking collectives: 1080 us -> 35.4 us
  waiting for transfers between devices: 138 us -> 695 us
  other arithmetic: 6.76 us -> 26.6 us
    psum x8 -> x0, blocking collectives: 1040 us -> none  [edge_table(): return lax.psum(local, 'tile')]
    all_gather x0 -> x8, waiting for transfers between devices: none -> 594 us  [edge_table(): return jnp.sum(lax.all_gather(local, 'tile'), axis=0)]
    psum x1, waiting for transfers between devices: 131 us -> 101 us  [body(): summed, weight_sum = lax.psum((weighted, weight_local), 'member')]
  transfers between devices with their start and end apart: 17 -> 25, of which waited for: 5 -> 9; matrix products, arithmetic and copies ran while one was open for 1% -> 4% of each run, Pallas kernels for 0% -> 0%
where the time goes in v1:
time: 865 us; the launch traced here: 864 us
  waiting for transfers between devices  695 us (80%)
  starting transfers between devices  57.3 us (7%)
  blocking collectives  35.4 us (4%)
  local copies, waits for them, and re-layouts  27.6 us (3%)
  other arithmetic  26.6 us (3%)
  between operations  15.5 us (2%)
    all_gather x8, waiting for transfers between devices, edge_table(): return jnp.sum(lax.all_gather(local, 'tile'), axis=0)  594 us
    psum x1, waiting for transfers between devices, body(): summed, weight_sum = lax.psum((weighted, weight_local), 'member')  101 us
    ppermute x8, starting transfers between devices, with_halo(): lax.ppermute(lax.slice_in_dim(block, 0, width, axis=dim), axis, backward)  39.9 us
    psum x1, blocking collectives, body(): summed, weight_sum = lax.psum((weighted, weight_local), 'member')  35.4 us
  transfers between devices with their start and end apart: 25, of which 9 were waited for; matrix products, arithmetic and copies ran while one was open for 4% of the time, Pallas kernels for 0%

profile of v1, /device:TPU:4, one launch (start us, length us, event | category | flops | bytes accessed | tf_op | source)
XLA Modules:
  0.0 864.1 jit_solution(2426476949947533295)
XLA Ops:
  7.2 1.0 slice_reduce_fusion.1
  8.2 1.1 copy.183
  9.4 1.0 dynamic_update_slice.24
  11.2 1.9 collective-permute-start
  13.1 5.1 collective-permute-start.1
  18.2 0.9 add_bitcast_fusion
  19.1 0.8 compare_bitcast_fusion
  20.1 79.1 %all-gather.17.cloned.1.call-done = f32[32,6,4,512]{3,2,1,0:T(4,128)} async-done(((f32[1,6,4,512]{3,2,1,0:T(4,128)}), f32[32,6,4,512]{3,2,1,0:T(4,128)}) %all-gather.17.cloned.1.call-update) | async-done | bytes 1572880 | tf_op jit(solution)/shard_map/all_gather | solution.py:45
  99.2 1.6 reduce.8
  103.9 1.0 dynamic_update_slice.25
  105.6 2.2 collective-permute-start.2
  107.8 4.9 collective-permute-start.3
  112.9 73.7 %all-gather.19.cloned.1.call-done = f32[32,6,4,512]{3,2,1,0:T(4,128)} async-done(((f32[1,6,4,512]{3,2,1,0:T(4,128)}), f32[32,6,4,512]{3,2,1,0:T(4,128)}) %all-gather.19.cloned.1.call-update) | async-done | bytes 1572880 | tf_op jit(solution)/shard_map/all_gather | solution.py:45
  186.6 1.6 reduce.9
  191.4 1.0 dynamic_update_slice.26
  193.1 2.2 collective-permute-start.4
  195.3 4.9 collective-permute-start.5
  200.4 73.7 %all-gather.21.cloned.1.call-done = f32[32,6,4,512]{3,2,1,0:T(4,128)} async-done(((f32[1,6,4,512]{3,2,1,0:T(4,128)}), f32[32,6,4,512]{3,2,1,0:T(4,128)}) %all-gather.21.cloned.1.call-update) | async-done | bytes 1572880 | tf_op jit(solution)/shard_map/all_gather | solution.py:45
  274.1 1.6 reduce.10
  278.8 1.0 dynamic_update_slice.27
  280.6 2.2 collective-permute-start.6
  282.8 5.0 collective-permute-start.7
  288.0 73.6 %all-gather.23.cloned.1.call-done = f32[32,6,4,512]{3,2,1,0:T(4,128)} async-done(((f32[1,6,4,512]{3,2,1,0:T(4,128)}), f32[32,6,4,512]{3,2,1,0:T(4,128)}) %all-gather.23.cloned.1.call-update) | async-done | bytes 1572880 | tf_op jit(solution)/shard_map/all_gather | solution.py:45
  361.6 1.6 reduce.11
  366.4 1.0 dynamic_update_slice.28
  368.2 2.2 collective-permute-start.8
  370.4 4.9 collective-permute-start.9
  375.4 73.7 %all-gather.25.cloned.1.call-done = f32[32,6,4,512]{3,2,1,0:T(4,128)} async-done(((f32[1,6,4,512]{3,2,1,0:T(4,128)}), f32[32,6,4,512]{3,2,1,0:T(4,128)}) %all-gather.25.cloned.1.call-update) | async-done | bytes 1572880 | tf_op jit(solution)/shard_map/all_gather | solution.py:45
  449.1 1.6 reduce.12
  453.9 1.0 dynamic_update_slice.29
  455.7 2.2 collective-permute-start.10
  457.8 4.9 collective-permute-start.11
  462.9 73.7 %all-gather.27.cloned.1.call-done = f32[32,6,4,512]{3,2,1,0:T(4,128)} async-done(((f32[1,6,4,512]{3,2,1,0:T(4,128)}), f32[32,6,4,512]{3,2,1,0:T(4,128)}) %all-gather.27.cloned.1.call-update) | async-done | bytes 1572880 | tf_op jit(solution)/shard_map/all_gather | solution.py:45
  536.6 1.6 reduce.13
  541.4 1.0 dynamic_update_slice.30
  543.1 2.2 collective-permute-start.12
  545.3 5.1 collective-permute-start.13
  550.6 73.5 %all-gather.29.cloned.1.call-done = f32[32,6,4,512]{3,2,1,0:T(4,128)} async-done(((f32[1,6,4,512]{3,2,1,0:T(4,128)}), f32[32,6,4,512]{3,2,1,0:T(4,128)}) %all-gather.29.cloned.1.call-update) | async-done | bytes 1572880 | tf_op jit(solution)/shard_map/all_gather | solution.py:45
  624.1 1.6 reduce.14
  628.9 1.0 dynamic_update_slice.31
  631.3 2.2 collective-permute-start.14
  633.5 5.0 collective-permute-start.15
  638.6 72.9 %all-gather.31.cloned.1.call-done = f32[32,6,4,512]{3,2,1,0:T(4,128)} async-done(((f32[1,6,4,512]{3,2,1,0:T(4,128)}), f32[32,6,4,512]{3,2,1,0:T(4,128)}) %all-gather.31.cloned.1.call-update) | async-done | bytes 1572880 | tf_op jit(solution)/shard_map/all_gather | solution.py:45
  711.6 1.6 reduce.15
  715.8 1.0 multiply_bitcast_fusion
  716.8 35.4 %psum.15 = f32[]{:T(128)} all-reduce(f32[]{:T(128)} %bitcast.118), channel_id=1, replica_groups=mesh['member'=16,'tile'=32] {'member'}, use_global_device_ids=true, to_apply=%region_9.10 | all-reduce | flops 1 | bytes 8 | tf_op jit(solution)/shard_map/psum | solution.py:83
  752.9 101.3 %all-reduce.2.cloned.1.call-done = f32[6,16,512]{2,0,1:T(8,128)} async-done(((f32[6,16,512]{2,0,1:T(8,128)}), f32[6,16,512]{2,0,1:T(8,128)}) %all-reduce.2.cloned.1.call-update) | async-done | bytes 196624 | tf_op jit(solution)/shard_map/psum | solution.py:83
  854.2 1.8 fusion.42
  (262 shorter events, 33.0 us)
Async XLA Ops:
  7.2 92.0 %all-gather.17.cloned.1.call-start = ((), (), s32[]{:S(2)}) async-start(), calls=%async_computation.1 | async-start | bytes 1622016 | tf_op jit(solution)/shard_map/all_gather | solution.py:45
  11.1 175.5 %all-gather.19.cloned.1.call-start = ((), (), s32[]{:S(2)}) async-start(), calls=%async_computation.2 | async-start | bytes 1622016 | tf_op jit(solution)/shard_map/all_gather | solution.py:45
  11.2 91.2 %collective-permute-start = (f32[1,6,1,512]{3,1,2,0:T(8,128)S(1)}, f32[1,6,1,512]{3,1,2,0:T(8,128)S(1)}, u32[]{:S(2)}, u32[]{:S(2)}) collective-permute-start(f32[1,6,1,512]{3,1,2,0:T(8,128)S(1)} %get-tuple-element.76), channel_id=1, source_target_pairs={{0,1},{1,2},{2,3},{3,4},{4,5},{5,6},{6,7},{7,8},{8,9},{9,10},{10,1... | collective-permute-start | bytes 36872 | tf_op jit(solution)/shard_map/ppermute | solution.py:15
  13.1 90.1 %collective-permute-start.1 = (f32[1,6,1,512]{3,1,2,0:T(8,128)S(1)}, f32[1,6,1,512]{3,1,2,0:T(8,128)S(1)}, u32[]{:S(2)}, u32[]{:S(2)}) collective-permute-start(f32[1,6,1,512]{3,1,2,0:T(8,128)S(1)} %get-tuple-element.79), channel_id=1, source_target_pairs={{1,0},{2,1},{3,2},{4,3},{5,4},{6,5},{7,6},{8,7},{9,8},{10,9},{11,1... | collective-permute-start | bytes 36872 | tf_op jit(solution)/shard_map/ppermute | solution.py:18
  105.6 168.5 %all-gather.21.cloned.1.call-start = ((), (), s32[]{:S(2)}) async-start(), calls=%async_computation.3 | async-start | bytes 1622016 | tf_op jit(solution)/shard_map/all_gather | solution.py:45
  105.6 84.2 %collective-permute-start.2 = (f32[1,6,1,512]{3,1,2,0:T(8,128)S(1)}, f32[1,6,1,512]{3,1,2,0:T(8,128)S(1)}, u32[]{:S(2)}, u32[]{:S(2)}) collective-permute-start(f32[1,6,1,512]{3,1,2,0:T(8,128)S(1)} %get-tuple-element.68), channel_id=1, source_target_pairs={{0,1},{1,2},{2,3},{3,4},{4,5},{5,6},{6,7},{7,8},{8,9},{9,10},{10,1... | collective-permute-start | bytes 36872 | tf_op jit(solution)/shard_map/ppermute | solution.py:15
  107.8 82.9 %collective-permute-start.3 = (f32[1,6,1,512]{3,1,2,0:T(8,128)S(1)}, f32[1,6,1,512]{3,1,2,0:T(8,128)S(1)}, u32[]{:S(2)}, u32[]{:S(2)}) collective-permute-start(f32[1,6,1,512]{3,1,2,0:T(8,128)S(1)} %get-tuple-element.71), channel_id=1, source_target_pairs={{1,0},{2,1},{3,2},{4,3},{5,4},{6,5},{7,6},{8,7},{9,8},{10,9},{11,1... | collective-permute-start | bytes 36872 | tf_op jit(solution)/shard_map/ppermute | solution.py:18
  193.1 168.5 %all-gather.23.cloned.1.call-start = ((), (), s32[]{:S(2)}) async-start(), calls=%async_computation.4 | async-start | bytes 1622016 | tf_op jit(solution)/shard_map/all_gather | solution.py:45
  193.1 84.2 %collective-permute-start.4 = (f32[1,6,1,512]{3,1,2,0:T(8,128)S(1)}, f32[1,6,1,512]{3,1,2,0:T(8,128)S(1)}, u32[]{:S(2)}, u32[]{:S(2)}) collective-permute-start(f32[1,6,1,512]{3,1,2,0:T(8,128)S(1)} %get-tuple-element.60), channel_id=1, source_target_pairs={{0,1},{1,2},{2,3},{3,4},{4,5},{5,6},{6,7},{7,8},{8,9},{9,10},{10,1... | collective-permute-start | bytes 36872 | tf_op jit(solution)/shard_map/ppermute | solution.py:15
  195.3 82.9 %collective-permute-start.5 = (f32[1,6,1,512]{3,1,2,0:T(8,128)S(1)}, f32[1,6,1,512]{3,1,2,0:T(8,128)S(1)}, u32[]{:S(2)}, u32[]{:S(2)}) collective-permute-start(f32[1,6,1,512]{3,1,2,0:T(8,128)S(1)} %get-tuple-element.63), channel_id=1, source_target_pairs={{1,0},{2,1},{3,2},{4,3},{5,4},{6,5},{7,6},{8,7},{9,8},{10,9},{11,1... | collective-permute-start | bytes 36872 | tf_op jit(solution)/shard_map/ppermute | solution.py:18
  280.6 168.6 %all-gather.25.cloned.1.call-start = ((), (), s32[]{:S(2)}) async-start(), calls=%async_computation.5 | async-start | bytes 1622016 | tf_op jit(solution)/shard_map/all_gather | solution.py:45
  280.6 84.2 %collective-permute-start.6 = (f32[1,6,1,512]{3,1,2,0:T(8,128)S(1)}, f32[1,6,1,512]{3,1,2,0:T(8,128)S(1)}, u32[]{:S(2)}, u32[]{:S(2)}) collective-permute-start(f32[1,6,1,512]{3,1,2,0:T(8,128)S(1)} %get-tuple-element.52), channel_id=1, source_target_pairs={{0,1},{1,2},{2,3},{3,4},{4,5},{5,6},{6,7},{7,8},{8,9},{9,10},{10,1... | collective-permute-start | bytes 36872 | tf_op jit(solution)/shard_map/ppermute | solution.py:15
  282.8 83.0 %copy-start.1 = (f32[1,6,16,512]{3,2,1,0:T(8,128)S(1)}, f32[1,6,16,512]{3,2,1,0:T(8,128)}, u32[]{:S(2)}) copy-start(f32[1,6,16,512]{3,2,1,0:T(8,128)} %param.4) | copy-start | bytes 589828
  282.8 82.9 %collective-permute-start.7 = (f32[1,6,1,512]{3,1,2,0:T(8,128)S(1)}, f32[1,6,1,512]{3,1,2,0:T(8,128)S(1)}, u32[]{:S(2)}, u32[]{:S(2)}) collective-permute-start(f32[1,6,1,512]{3,1,2,0:T(8,128)S(1)} %get-tuple-element.55), channel_id=1, source_target_pairs={{1,0},{2,1},{3,2},{4,3},{5,4},{6,5},{7,6},{8,7},{9,8},{10,9},{11,1... | collective-permute-start | bytes 36872 | tf_op jit(solution)/shard_map/ppermute | solution.py:18
  368.1 168.5 %all-gather.27.cloned.1.call-start = ((), (), s32[]{:S(2)}) async-start(), calls=%async_computation.6 | async-start | bytes 1622016 | tf_op jit(solution)/shard_map/all_gather | solution.py:45
  368.2 84.2 %collective-permute-start.8 = (f32[1,6,1,512]{3,1,2,0:T(8,128)S(1)}, f32[1,6,1,512]{3,1,2,0:T(8,128)S(1)}, u32[]{:S(2)}, u32[]{:S(2)}) collective-permute-start(f32[1,6,1,512]{3,1,2,0:T(8,128)S(1)} %get-tuple-element.44), channel_id=1, source_target_pairs={{0,1},{1,2},{2,3},{3,4},{4,5},{5,6},{6,7},{7,8},{8,9},{9,10},{10,1... | collective-permute-start | bytes 36872 | tf_op jit(solution)/shard_map/ppermute | solution.py:15
  370.4 82.9 %collective-permute-start.9 = (f32[1,6,1,512]{3,1,2,0:T(8,128)S(1)}, f32[1,6,1,512]{3,1,2,0:T(8,128)S(1)}, u32[]{:S(2)}, u32[]{:S(2)}) collective-permute-start(f32[1,6,1,512]{3,1,2,0:T(8,128)S(1)} %get-tuple-element.47), channel_id=1, source_target_pairs={{1,0},{2,1},{3,2},{4,3},{5,4},{6,5},{7,6},{8,7},{9,8},{10,9},{11,1... | collective-permute-start | bytes 36872 | tf_op jit(solution)/shard_map/ppermute | solution.py:18
  455.6 168.5 %all-gather.29.cloned.1.call-start = ((), (), s32[]{:S(2)}) async-start(), calls=%async_computation.7 | async-start | bytes 1622016 | tf_op jit(solution)/shard_map/all_gather | solution.py:45
  455.7 84.2 %collective-permute-start.10 = (f32[1,6,1,512]{3,1,2,0:T(8,128)S(1)}, f32[1,6,1,512]{3,1,2,0:T(8,128)S(1)}, u32[]{:S(2)}, u32[]{:S(2)}) collective-permute-start(f32[1,6,1,512]{3,1,2,0:T(8,128)S(1)} %get-tuple-element.36), channel_id=1, source_target_pairs={{0,1},{1,2},{2,3},{3,4},{4,5},{5,6},{6,7},{7,8},{8,9},{9,10},{10,1... | collective-permute-start | bytes 36872 | tf_op jit(solution)/shard_map/ppermute | solution.py:15
  457.8 82.9 %collective-permute-start.11 = (f32[1,6,1,512]{3,1,2,0:T(8,128)S(1)}, f32[1,6,1,512]{3,1,2,0:T(8,128)S(1)}, u32[]{:S(2)}, u32[]{:S(2)}) collective-permute-start(f32[1,6,1,512]{3,1,2,0:T(8,128)S(1)} %get-tuple-element.39), channel_id=1, source_target_pairs={{1,0},{2,1},{3,2},{4,3},{5,4},{6,5},{7,6},{8,7},{9,8},{10,9},{11,1... | collective-permute-start | bytes 36872 | tf_op jit(solution)/shard_map/ppermute | solution.py:18
  543.1 168.5 %all-gather.31.cloned.1.call-start = ((), (), s32[]{:S(2)}) async-start(), calls=%async_computation.8 | async-start | bytes 1622016 | tf_op jit(solution)/shard_map/all_gather | solution.py:45
  543.1 84.2 %collective-permute-start.12 = (f32[1,6,1,512]{3,1,2,0:T(8,128)S(1)}, f32[1,6,1,512]{3,1,2,0:T(8,128)S(1)}, u32[]{:S(2)}, u32[]{:S(2)}) collective-permute-start(f32[1,6,1,512]{3,1,2,0:T(8,128)S(1)} %get-tuple-element.28), channel_id=1, source_target_pairs={{0,1},{1,2},{2,3},{3,4},{4,5},{5,6},{6,7},{7,8},{8,9},{9,10},{10,1... | collective-permute-start | bytes 36872 | tf_op jit(solution)/shard_map/ppermute | solution.py:15
  545.3 82.9 %collective-permute-start.13 = (f32[1,6,1,512]{3,1,2,0:T(8,128)S(1)}, f32[1,6,1,512]{3,1,2,0:T(8,128)S(1)}, u32[]{:S(2)}, u32[]{:S(2)}) collective-permute-start(f32[1,6,1,512]{3,1,2,0:T(8,128)S(1)} %get-tuple-element.31), channel_id=1, source_target_pairs={{1,0},{2,1},{3,2},{4,3},{5,4},{6,5},{7,6},{8,7},{9,8},{10,9},{11,1... | collective-permute-start | bytes 36872 | tf_op jit(solution)/shard_map/ppermute | solution.py:18
  630.6 223.6 %all-reduce.2.cloned.1.call-start = ((), (), s32[]{:S(2)}) async-start(), calls=%async_computation | async-start | bytes 524288 | tf_op jit(solution)/shard_map/psum | solution.py:83
  631.3 83.6 %collective-permute-start.14 = (f32[1,6,1,512]{3,1,2,0:T(8,128)S(1)}, f32[1,6,1,512]{3,1,2,0:T(8,128)S(1)}, u32[]{:S(2)}, u32[]{:S(2)}) collective-permute-start(f32[1,6,1,512]{3,1,2,0:T(8,128)S(1)} %get-tuple-element.18), channel_id=1, source_target_pairs={{0,1},{1,2},{2,3},{3,4},{4,5},{5,6},{6,7},{7,8},{8,9},{9,10},{10,1... | collective-permute-start | bytes 36872 | tf_op jit(solution)/shard_map/ppermute | solution.py:15
  633.5 82.3 %copy-start = (f32[1,6,16,512]{3,2,1,0:T(8,128)S(1)}, f32[1,6,16,512]{3,2,1,0:T(8,128)}, u32[]{:S(2)}) copy-start(f32[1,6,16,512]{3,2,1,0:T(8,128)} %param.5) | copy-start | bytes 589828
  633.5 82.2 %collective-permute-start.15 = (f32[1,6,1,512]{3,1,2,0:T(8,128)S(1)}, f32[1,6,1,512]{3,1,2,0:T(8,128)S(1)}, u32[]{:S(2)}, u32[]{:S(2)}) collective-permute-start(f32[1,6,1,512]{3,1,2,0:T(8,128)S(1)} %get-tuple-element.21), channel_id=1, source_target_pairs={{1,0},{2,1},{3,2},{4,3},{5,4},{6,5},{7,6},{8,7},{9,8},{10,9},{11,1... | collective-permute-start | bytes 36872 | tf_op jit(solution)/shard_map/ppermute | solution.py:18
Sparse Core Ops, SparseCore 0:
  11.9 87.2 all-gather.16
  105.7 80.8 all-gather.18
  193.2 80.8 all-gather.20
  280.7 80.8 all-gather.22
  368.2 80.8 all-gather.24
  455.7 80.8 all-gather.26
  543.2 80.8 all-gather.28
  630.7 80.8 all-gather.30
  716.9 137.2 all-reduce.1
